TPU v7x, 32 devices: a whole 2x2x4 slice. The times are simulated.
32 devices in a mesh: gx: 16 (over z, x, core), gz: 2 (over y).
Axes of the slice: x: 2, y: 2, z: 4, core: 2. Of those that a mesh axis runs over, the one named last changes fastest.
Arguments:
- velocity: float32 [8, 4, 2048, 512], P(None, None, 'gx', 'gz'), may hold values from -130 to 130
- kept: int32 [6], replicated, may hold values from 0 to 7, as said below
- shift: int32 [7], replicated, may hold values from 0 to 64, as said below
Outputs:
- correlation_map: float32 [7, 4, 2048, 512], P(None, None, 'gx', 'gz')
- coefficient: float32 [7, 4], replicated
Inputs may be any that keep to these rules, and one draw needn't show every extreme that they name: `kept`: 6 distinct snapshot indices in increasing order. `shift`: not falling with the separation; the shift of the longest separation is 64.
All inputs are finite; a program needn't handle non-finite values.
Results may differ from a plain program's by a relative error of at most 0.0001.
Values sent between devices are 32-bit elements; how exact they have to be, the bound alone decides.
A program may use at most 128 MiB of HBM per device.

v0:
```python
import functools
import math

import jax
import jax.numpy as jnp
from jax import lax
from jax.experimental import pallas as pl
from jax.experimental.pallas import tpu as pltpu
from jax.sharding import PartitionSpec as P

gauss_raw = [math.exp(-k * k / 8.0) for k in range(-4, 5)]
gauss_taps = [v / sum(gauss_raw) for v in gauss_raw]
MESH = pl.DeviceIdType.MESH
LANES = 128
REACH = 8
SIZES = []
f32 = jnp.float32
bf16 = jnp.bfloat16


def tap_of(distance):
    value = jnp.zeros(distance.shape, f32)
    for k in range(5):
        value = jnp.where(distance == k, gauss_taps[4 + k], value)
    return value


def halves(x):
    hi = x.astype(bf16)
    return hi, (x - hi.astype(f32)).astype(bf16)


def remote(src_ref, dst_ref, send, recv, dev):
    return pltpu.make_async_remote_copy(
        src_ref=src_ref, dst_ref=dst_ref, send_sem=send, recv_sem=recv,
        device_id=dev, device_id_type=MESH)


def summed(tile, zbuf, xbuf, rz_send, rz_recv, rx_send, rx_recv):
    gx, gz = lax.axis_index("gx"), lax.axis_index("gz")
    nx, nz = lax.axis_size("gx"), lax.axis_size("gz")
    zbuf[gz] = tile

    def z_copy(k, send):
        k = k if send else nz - k
        who = lax.rem(gz + k, nz)
        at = gz if send else who
        sem = k if send else nz - k
        return remote(zbuf.at[at], zbuf.at[at], rz_send.at[sem], rz_recv.at[sem], (gx, who))

    @pl.loop(1, nz)
    def _(k):
        z_copy(k, True).start()

    @pl.loop(1, nz)
    def _(k):
        z_copy(k, False).wait_recv()

    xbuf[gx] = jnp.sum(zbuf[...], axis=0)

    def x_copy(k, send):
        k = k if send else nx - k
        who = lax.rem(gx + k, nx)
        at = gx if send else who
        sem = k if send else nx - k
        return remote(xbuf.at[at], xbuf.at[at], rx_send.at[sem], rx_recv.at[sem], (who, gz))

    @pl.loop(1, nx)
    def _(k):
        x_copy(k, True).start()

    @pl.loop(1, nx)
    def _(k):
        x_copy(k, False).wait_recv()

    result = jnp.sum(xbuf[...], axis=0)

    @pl.loop(1, nz)
    def _(k):
        z_copy(k, True).wait_send()

    @pl.loop(1, nx)
    def _(k):
        x_copy(k, True).wait_send()

    return result


def taps_x(zb, c, at, size):
    y = gauss_taps[4] * zb[c, at : at + size, :]
    for k in range(1, 5):
        y = y + gauss_taps[4 + k] * (zb[c, at - k : at - k + size, :] + zb[c, at + k : at + k + size, :])
    return y


def exchange(tiles, cells, vel_hbm, kept, shift, fb_hbm, inv, pair_sum, vel, fb, tail, zx, hx,
             head_s, head_r, main_s, main_r, up_s, up_r, edge, zh, whi, wlo, zb, zc, eb,
             ez, ex, vel_sem, out_sem, x_send, x_recv, m_send, m_recv, z_send, z_recv,
             rz_send, rz_recv, rx_send, rx_recv):
    snaps, planes, deep, _, cols = vel.shape
    rows = 8 * deep
    wide = cols // LANES
    nk = kept.shape[0]
    nx, nz = lax.axis_size("gx"), lax.axis_size("gz")
    gx, gz = lax.axis_index("gx"), lax.axis_index("gz")
    xp, xm = lax.rem(gx + 1, nx), lax.rem(gx + nx - 1, nx)
    zp, zm = lax.rem(gz + 1, nz), lax.rem(gz + nz - 1, nz)

    barrier = pltpu.get_barrier_semaphore()

    def greet(dev):
        pl.semaphore_signal(barrier, inc=1, device_id=dev, device_id_type=MESH)

    for dev in ((xm, zm), (xm, zp), (xp, zm), (xp, zp)):
        greet(dev)

    @pl.loop(1, nx)
    def _(k):
        greet((lax.rem(gx + k, nx), gz))

    @pl.loop(1, nz)
    def _(k):
        greet((gx, lax.rem(gz + k, nz)))

    loads = [pltpu.make_async_copy(vel_hbm.at[t], vel.at[t], vel_sem.at[t]) for t in range(snaps)]
    for c in loads:
        c.start()

    src = lax.broadcasted_iota(jnp.int32, (cols + 2 * LANES, cols), 0)
    dst = lax.broadcasted_iota(jnp.int32, (cols + 2 * LANES, cols), 1)
    place = jnp.where(src < cols, src, jnp.where(src < cols + LANES, src % 4 - 4, cols + src % 4))
    weights = tap_of(jnp.abs(place - dst))
    hi, lo = halves(weights)
    whi[...] = hi
    wlo[...] = lo

    reach = []
    start = []
    total = jnp.int32(0)
    for j in range(1, nk):
        s = shift[jnp.clip(kept[j] - kept[0] - 1, 0, snaps - 2)]
        n = (s + 3) // 8
        start.append(total)
        reach.append(n)
        total = total + n

    def source(m):
        j = jnp.int32(1)
        base = start[0]
        for i in range(2, nk):
            later = m >= start[i - 1]
            j = jnp.where(later, i, j)
            base = jnp.where(later, start[i - 1], base)
        return j, jnp.clip(m - base + 1, 1, REACH)

    for c in loads:
        c.wait()

    low = lax.broadcasted_iota(jnp.int32, (8, cols), 0) < 4

    @pl.loop(0, nk)
    def _(j):
        t = kept[j]
        for p in range(planes):
            head_s[j * planes + p] = vel[t, p, 0]
        for p in range(0, planes, 2):
            even = vel[t, p, deep - 1]
            odd = vel[t, p + 1, deep - 1]
            up_s[j * (planes // 2) + p // 2] = jnp.where(low, pltpu.roll(even, 4, 0), odd)

    pl.semaphore_wait(barrier, nx - 1 + nz - 1 + 4)

    head = remote(head_s, head_r, x_send.at[0], x_recv.at[0], (xm, gz))
    head.start()
    upper = remote(up_s, up_r, x_send.at[1], x_recv.at[1], (xp, gz))
    upper.start()

    @pl.loop(0, tiles)
    def _(m):
        j, q = source(m)
        t = kept[j]
        for p in range(planes):
            main_s[p, m] = vel[t, p, q]

    mains = [remote(main_s.at[p], main_r.at[p], m_send.at[p], m_recv.at[p], (xm, gz)) for p in range(planes)]
    mains[0].start()

    lane = lax.broadcasted_iota(jnp.int32, (rows, LANES), 1)
    edge[...] = jnp.zeros(edge.shape, f32)

    @pl.loop(0, nk)
    def _(j):
        t = kept[j]
        left, right = edge[0].reshape(rows, LANES), edge[1].reshape(rows, LANES)
        for p in range(planes):
            m = j * planes + p
            mine = lane // 4 == m
            block = vel[t, p].reshape(rows, cols)
            left = jnp.where(mine, pltpu.roll(block[:, :LANES], 4 * m, 1), left)
            right = jnp.where(mine, pltpu.roll(block[:, cols - LANES :], 4 * m + 4, 1), right)
        edge[0] = left.reshape(deep, 8, LANES)
        edge[1] = right.reshape(deep, 8, LANES)

    zs = []
    for side, (e, dz) in enumerate(((1, zp), (0, zm))):
        for n, (dx, a, size, at) in enumerate(((gx, 0, deep, 1), (xm, 0, REACH + 1, 1 + deep), (xp, deep - 1, 1, 0))):
            zs.append(remote(edge.at[e, pl.ds(a, size)], zh.at[side, pl.ds(at, size)],
                             z_send.at[3 * side + n], z_recv.at[3 * side + n], (dx, dz)))
    for c in zs:
        c.start()
    for c in mains[1:]:
        c.start()

    def along_z(x, sides, mine):
        sides = [jnp.where(mine, side.reshape(x.shape[0], LANES), 0.0) for side in sides]
        a, b = halves(jnp.concatenate([x] + sides, axis=1))
        dot = functools.partial(jnp.dot, preferred_element_type=f32)
        return dot(a, whi[...]) + dot(b, whi[...]) + dot(a, wlo[...])

    head.wait_recv()
    upper.wait_recv()
    for c in zs:
        c.wait_recv()

    @pl.loop(0, nk)
    def _(j):
        t = kept[j]
        for p in range(planes):
            m = j * planes + p
            tile = up_r[j * (planes // 2) + p // 2]
            tile = tile if p % 2 == 1 else pltpu.roll(tile, 4, 0)
            x = jnp.concatenate([tile, vel[t, p].reshape(rows, cols), head_r[m]], axis=0)
            mine = lax.broadcasted_iota(jnp.int32, (rows + 16, LANES), 1) // 4 == m
            y = along_z(x, [zh[side, : deep + 2] for side in range(2)], mine)
            for c in range(wide):
                zb[p, c] = y[:, c * LANES : (c + 1) * LANES]
                tail[m, c] = y[rows:, c * LANES : (c + 1) * LANES]
        for p in range(planes):
            m = j * planes + p
            energy = jnp.zeros((1, LANES), f32)
            for c in range(wide):
                y = taps_x(zb.at[p], c, 8, rows)
                fb[m, c, :deep] = y.reshape(deep, 8, LANES)
                energy = energy + jnp.sum(y * y, axis=0, keepdims=True)
            eb[pl.ds(m, 1), :] = energy

    lane8 = lax.broadcasted_iota(jnp.int32, (8, LANES), 1)

    @pl.loop(0, tiles)
    def _(m):
        j, q = source(m)
        mine = lane8 // (4 * planes) == j
        for side in range(2):
            hx[side, m] = jnp.where(mine, zh[side, deep + 1 + q], 0.0)

    owner = lax.broadcasted_iota(jnp.int32, (8 * tiles, LANES), 1) // 4 % planes
    sub = lax.broadcasted_iota(jnp.int32, (deep, 8, LANES), 1)
    pairs = [(a, b) for a in range(nk) for b in range(a + 1, nk)]
    eb[pl.ds(nk * planes + len(pairs) * planes, 4), :] = jnp.zeros((4, LANES), f32)

    @pl.loop(0, planes)
    def _(p):
        remote(main_s.at[p], main_r.at[p], m_send.at[p], m_recv.at[p], (xm, gz)).wait_recv()
        y = along_z(main_r[p].reshape(8 * tiles, cols), [hx[0], hx[1]], owner == p)
        for c in range(wide):
            zx[c] = y[:, c * LANES : (c + 1) * LANES].reshape(tiles, 8, LANES)
        for j in range(1, nk):
            m = j * planes + p
            for c in range(wide):
                zc[j - 1, c, 0:16, :] = tail[m, c]
                for q in range(1, REACH + 1):
                    at = start[j - 1] + jnp.clip(q, 1, jnp.maximum(reach[j - 1], 1)) - 1
                    zc[j - 1, c, 8 + 8 * q : 16 + 8 * q, :] = zx[c, jnp.clip(at, 0, tiles - 1)]
            for c in range(wide):
                fb[m, c, deep:] = taps_x(zc.at[j - 1], c, 8, 8 * REACH).reshape(REACH, 8, LANES)
        for n, (a, b) in enumerate(pairs):
            s = shift[jnp.clip(kept[b] - kept[a] - 1, 0, snaps - 2)]
            whole, rest = s // 8, s % 8
            total = jnp.zeros((8, LANES), f32)
            for c in range(wide):
                later = jnp.stack([fb[b * planes + p, c, jnp.clip(q + whole, 0, deep + REACH - 1)]
                                   for q in range(deep + 1)])
                later = pltpu.roll(later, (8 - rest) % 8, 1)
                later = jnp.where(sub < 8 - rest, later[:deep], later[1:])
                total = total + jnp.sum(fb[a * planes + p, c, :deep] * later, axis=0)
            eb[pl.ds(planes * (nk + n) + p, 1), :] = jnp.sum(total, axis=0, keepdims=True)

    local = pltpu.make_async_copy(fb, fb_hbm, out_sem.at[0])
    local.start()
    tile = jnp.zeros((8, LANES), f32)
    groups = eb.shape[0] // 8
    for g in range(groups):
        part = jnp.sum(eb[8 * g : 8 * g + 8, :], axis=1, keepdims=True)
        tile = jnp.where(lane8 == g, part, tile)
    tile = summed(tile, ez, ex, rz_send, rz_recv, rx_send, rx_recv)
    for g in range(groups):
        mean = jnp.sum(jnp.where(lane8 == g, tile, 0.0), axis=1, keepdims=True) / cells
        mean = jnp.broadcast_to(mean, (8, LANES))
        if 8 * g < nk * planes:
            inv[8 * g : 8 * g + 8, :] = 1.0 / jnp.sqrt(mean + 1e-06)
        else:
            at = 8 * g - nk * planes
            pair_sum[at : at + 8, :] = mean

    head.wait_send()
    upper.wait_send()
    for c in zs:
        c.wait_send()
    for c in mains:
        c.wait_send()
    local.wait()


def correlate(kept, shift, fb, inv, pair_sum, out, coef, pairs, number):
    nk, _, wide, _, _ = fb.shape
    rows = out.shape[2]
    lags = shift.shape[0]
    p = pl.program_id(0)
    planes = pl.num_programs(0)

    @pl.when(p == 0)
    def _():
        for d in range(lags):
            number[d] = 0
        n = 0
        for i in range(nk):
            for j in range(i + 1, nk):
                d = jnp.clip(kept[j] - kept[i] - 1, 0, lags - 1)
                pairs[d, number[d]] = 64 * n + 8 * i + j
                number[d] = number[d] + 1
                n += 1

    lane = lax.broadcasted_iota(jnp.int32, (1, LANES), 1)
    means = jnp.zeros((1, LANES), f32)
    for d in range(lags):
        n = number[d]
        s = shift[d]
        share = 1.0 / jnp.maximum(n, 1).astype(f32)

        def add(i, carry):
            code = pairs[d, i]
            a, b = code // 8 % 8, code % 8
            scale = inv[pl.ds(a * planes + p, 1), :] * inv[pl.ds(b * planes + p, 1), :] * share
            mean = carry[0] + pair_sum[pl.ds(code // 64 * planes + p, 1), :] * scale
            return (mean,) + tuple(
                carry[1 + c] + (fb[a, 0, c, :rows, :] * scale) * fb[b, 0, c, pl.ds(s, rows), :] for c in range(wide))

        zero = jnp.zeros((rows, LANES), f32)
        mean, *maps = lax.fori_loop(0, n, add, (jnp.zeros((1, LANES), f32),) + (zero,) * wide)
        for c in range(wide):
            out[d, 0, :, c * LANES : (c + 1) * LANES] = maps[c]
        means = jnp.where(lane == d, mean, means)
    coef[pl.ds(p, 1), :] = means[:, :lags]


def on_device(velocity, kept, shift):
    snaps, planes, rows, cols = velocity.shape
    nk = kept.shape[0]
    nx, nz = lax.axis_size("gx"), lax.axis_size("gz")
    cells = rows * nx * cols * nz
    n = nk * planes
    deep = rows // 8
    wide = cols // LANES
    dma = pltpu.SemaphoreType.DMA
    vmem = pl.BlockSpec(memory_space=pltpu.VMEM)
    smem = pl.BlockSpec(memory_space=pltpu.SMEM)
    anywhere = pl.BlockSpec(memory_space=pl.ANY)
    shape = jax.ShapeDtypeStruct
    tiled = velocity.reshape(snaps, planes, deep, 8, cols)
    count = planes * nk * (nk - 1) // 2
    sums = -(-(n + count) // 8) * 8

    def exchanged(tiles, number):
        return pl.pallas_call(
            functools.partial(exchange, tiles, cells),
            out_shape=(shape((n, wide, deep + REACH, 8, LANES), f32), shape((n, LANES), f32),
                       shape((sums - n, LANES), f32)),
            in_specs=[anywhere, smem, smem],
            out_specs=(anywhere, vmem, vmem),
            scratch_shapes=[
                pltpu.VMEM((snaps, planes, deep, 8, cols), f32),
                pltpu.VMEM((n, wide, deep + REACH, 8, LANES), f32),
                pltpu.VMEM((n, wide, 16, LANES), f32),
                pltpu.VMEM((wide, tiles, 8, LANES), f32),
                pltpu.VMEM((2, tiles, 8, LANES), f32),
                pltpu.VMEM((n, 8, cols), f32),
                pltpu.VMEM((n, 8, cols), f32),
                pltpu.VMEM((planes, tiles, 8, cols), f32),
                pltpu.VMEM((planes, tiles, 8, cols), f32),
                pltpu.VMEM((n // 2, 8, cols), f32),
                pltpu.VMEM((n // 2, 8, cols), f32),
                pltpu.VMEM((2, deep, 8, LANES), f32),
                pltpu.VMEM((2, deep + REACH + 2, 8, LANES), f32),
                pltpu.VMEM((cols + 2 * LANES, cols), bf16),
                pltpu.VMEM((cols + 2 * LANES, cols), bf16),
                pltpu.VMEM((planes, wide, rows + 16, LANES), f32),
                pltpu.VMEM((nk - 1, wide, 16 + 8 * REACH, LANES), f32),
                pltpu.VMEM((sums, LANES), f32),
                pltpu.VMEM((nz, 8, LANES), f32),
                pltpu.VMEM((nx, 8, LANES), f32),
                dma((snaps,)), dma((1,)),
                dma((2,)), dma((2,)), dma((planes,)), dma((planes,)), dma((6,)), dma((6,)),
                dma((nz,)), dma((nz,)), dma((nx,)), dma((nx,)),
            ],
            compiler_params=pltpu.CompilerParams(
                collective_id=number, has_side_effects=True, vmem_limit_bytes=48 * 1024 * 1024),
        )

    sizes = SIZES + [(nk - 1) * REACH]
    needed = jnp.int32(0)
    for d in range(1, snaps):
        inside = jnp.any(kept - kept[0] == d)
        needed = needed + jnp.where(inside, (shift[d - 1] + 3) >> 3, 0)
    branch = sum((needed > size).astype(jnp.int32) for size in sizes[:-1])
    if len(sizes) == 1:
        fb, inv, pair_sum = exchanged(sizes[0], 0)(tiled, kept, shift)
    else:
        fb, inv, pair_sum = lax.switch(
            branch, [exchanged(size, number) for number, size in enumerate(sizes)], tiled, kept, shift)
    maps, coefficient = pl.pallas_call(
        correlate,
        grid=(planes,),
        out_shape=(shape((snaps - 1, planes, rows, cols), f32), shape((planes, snaps - 1), f32)),
        in_specs=[smem, smem,
                  pl.BlockSpec((nk, 1, wide, rows + 8 * REACH, LANES), lambda p: (0, p, 0, 0, 0)),
                  pl.BlockSpec((n, LANES), lambda p: (0, 0)),
                  pl.BlockSpec((sums - n, LANES), lambda p: (0, 0))],
        out_specs=(pl.BlockSpec((snaps - 1, 1, rows, cols), lambda p: (0, p, 0, 0)),
                   pl.BlockSpec((planes, snaps - 1), lambda p: (0, 0))),
        scratch_shapes=[pltpu.SMEM((8, 16), jnp.int32), pltpu.SMEM((8,), jnp.int32)],
        compiler_params=pltpu.CompilerParams(vmem_limit_bytes=48 * 1024 * 1024),
    )(kept, shift, fb.reshape(nk, planes, wide, rows + 8 * REACH, LANES), inv, pair_sum)
    return maps, coefficient.T


def solution(mesh):
    return jax.shard_map(
        on_device,
        mesh=mesh,
        in_specs=(P(None, None, "gx", "gz"), P(), P()),
        out_specs=(P(None, None, "gx", "gz"), P()),
        check_vma=False,
    )
```

profile of v0, /device:TPU:0, one launch (start us, length us, event | category | flops | bytes accessed | tf_op | source)
XLA Modules:
  0.0 57.2 jit_solution(8511387784734927228)
XLA Ops:
  0.6 0.0 copy-start.5
  0.6 0.0 copy-start.3
  0.6 0.0 copy-start.1
  0.7 2.2 %copy-done.1 = f32[8,4,128,256]{3,2,1,0:T(8,128)S(1)} copy-done((f32[8,4,128,256]{3,2,1,0:T(8,128)S(1)}, f32[8,4,128,256]{3,2,1,0:T(8,128)}, u32[]{:S(2)}) %copy-start.1) | copy-done | bytes 4194328
  2.9 0.0 copy-start.2
  2.9 0.7 %copy-done.2 = s32[6]{0:T(128)S(1)} copy-done((s32[6]{0:T(128)S(1)}, s32[6]{0:T(128)}, u32[]{:S(2)}) %copy-start.2) | copy-done | bytes 48
  3.5 0.0 copy-start.4
  3.5 0.7 %copy-done.4 = s32[7]{0:T(128)S(1)} copy-done((s32[7]{0:T(128)S(1)}, s32[7]{0:T(128)}, u32[]{:S(2)}) %copy-start.4) | copy-done | bytes 52
  4.2 44.8 %shard_map.50 = (f32[24,2,24,8,128]{4,3,2,1,0:T(8,128)}, f32[24,128]{1,0:T(8,128)S(1)}, f32[64,128]{1,0:T(8,128)S(1)}) custom-call(f32[8,4,16,8,256]{4,3,2,1,0:T(8,128)S(1)} %bitcast.4, s32[6]{0:T(128)S(1)} %copy-done.2, s32[7]{0:T(128)S(1)} %copy-done.4), custom_call_target="tpu_custom_call" | custom-call | tf_op jit(solution)/shard_map/pallas_call | solution.py:416
  49.0 0.0 copy-done.5
  49.0 0.0 copy-done.3
  49.0 0.0 copy-start
  49.0 2.3 %copy-done = f32[24,2,24,8,128]{4,3,2,1,0:T(8,128)S(1)} copy-done((f32[24,2,24,8,128]{4,3,2,1,0:T(8,128)S(1)}, f32[24,2,24,8,128]{4,3,2,1,0:T(8,128)}, u32[]{:S(2)}) %copy-start) | copy-done | bytes 4718616
  51.3 5.8 %shard_map.51 = (f32[7,4,128,256]{3,2,1,0:T(8,128)}, f32[4,7]{1,0:T(4,128)}) custom-call(s32[6]{0:T(128)S(1)} %copy-done.3, s32[7]{0:T(128)S(1)} %copy-done.5, f32[6,4,2,192,128]{4,3,2,1,0:T(8,128)S(1)} %bitcast.3, f32[24,128]{1,0:T(8,128)S(1)} %get-tuple-element.8.inv, f32[64,128]{1,0:T(8,128)S(1)} %get-tuple-element.9.pair_sum), custom_call_target="tpu_custom_call" | custom-call | tf_op jit(solution)/shard_map/pallas_call | solution.py:420
Async XLA Ops:
  0.6 48.3 %copy-start.5 = (s32[7]{0:T(128)S(1)}, s32[7]{0:T(128)}, u32[]{:S(2)}) copy-start(s32[7]{0:T(128)} %shift.3) | copy-start | bytes 88
  0.6 48.3 %copy-start.3 = (s32[6]{0:T(128)S(1)}, s32[6]{0:T(128)}, u32[]{:S(2)}) copy-start(s32[6]{0:T(128)} %kept.3) | copy-start | bytes 76
  0.6 2.2 %copy-start.1 = (f32[8,4,128,256]{3,2,1,0:T(8,128)S(1)}, f32[8,4,128,256]{3,2,1,0:T(8,128)}, u32[]{:S(2)}) copy-start(f32[8,4,128,256]{3,2,1,0:T(8,128)} %param.3) | copy-start | bytes 12582916
  2.9 0.7 %copy-start.2 = (s32[6]{0:T(128)S(1)}, s32[6]{0:T(128)}, u32[]{:S(2)}) copy-start(s32[6]{0:T(128)} %kept.3) | copy-start | bytes 76
  3.5 0.7 %copy-start.4 = (s32[7]{0:T(128)S(1)}, s32[7]{0:T(128)}, u32[]{:S(2)}) copy-start(s32[7]{0:T(128)} %shift.3) | copy-start | bytes 88
  49.0 2.3 %copy-start = (f32[24,2,24,8,128]{4,3,2,1,0:T(8,128)S(1)}, f32[24,2,24,8,128]{4,3,2,1,0:T(8,128)}, u32[]{:S(2)}) copy-start(f32[24,2,24,8,128]{4,3,2,1,0:T(8,128)} %get-tuple-element.7) | copy-start | bytes 14155780
where the time goes:
time: 57.4 us; the launch traced here: 57.2 us
  Pallas kernels  50.6 us (88%)
  local copies, waits for them, and re-layouts  5.84 us (10%)
  between operations  0.69 us (1%)
    pallas_call x1, Pallas kernels, on_device(): fb, inv, pair_sum = exchanged(sizes[0], 0)(tiled, kept, shift)  44.8 us
    unnamed x12, local copies, waits for them, and re-layouts  5.84 us
    pallas_call x1, Pallas kernels, on_device(): pl.pallas_call(correlate, grid=(planes,), out_shape=(shape((snaps - 1, pl...  5.82 us

commit v1 on v0

--- a/solution.py
+++ b/solution.py
@@ -403,7 +403,7 @@
                 dma((nz,)), dma((nz,)), dma((nx,)), dma((nx,)),
             ],
             compiler_params=pltpu.CompilerParams(
-                collective_id=number, has_side_effects=True, vmem_limit_bytes=48 * 1024 * 1024),
+                collective_id=number, has_side_effects=True, vmem_limit_bytes=60 * 1024 * 1024),
         )
 
     sizes = SIZES + [(nk - 1) * REACH]
@@ -428,7 +428,7 @@
         out_specs=(pl.BlockSpec((snaps - 1, 1, rows, cols), lambda p: (0, p, 0, 0)),
                    pl.BlockSpec((planes, snaps - 1), lambda p: (0, 0))),
         scratch_shapes=[pltpu.SMEM((8, 16), jnp.int32), pltpu.SMEM((8,), jnp.int32)],
-        compiler_params=pltpu.CompilerParams(vmem_limit_bytes=48 * 1024 * 1024),
+        compiler_params=pltpu.CompilerParams(vmem_limit_bytes=60 * 1024 * 1024),
     )(kept, shift, fb.reshape(nk, planes, wide, rows + 8 * REACH, LANES), inv, pair_sum)
     return maps, coefficient.T
 

time: 57.4 us -> 53.3 us (0.929)
  local copies, waits for them, and re-layouts: 5.84 us -> 0 us
  Pallas kernels: 50.6 us -> 52.5 us
    unnamed x12 -> x0, local copies, waits for them, and re-layouts: 5.84 us -> none
    pallas_call x1, Pallas kernels: 5.82 us -> 7.05 us  [on_device(): pl.pallas_call(correlate, grid=(planes,), out_shape=(shape((snaps - 1, pl...]
    pallas_call x1, Pallas kernels: 44.8 us -> 45.4 us  [on_device(): fb, inv, pair_sum = exchanged(sizes[0], 0)(tiled, kept, shift)]
where the time goes in v1:
time: 53.3 us; the launch traced here: 53.1 us
  Pallas kernels  52.5 us (98%)
  between operations  0.64 us (1%)
    pallas_call x1, Pallas kernels, on_device(): fb, inv, pair_sum = exchanged(sizes[0], 0)(tiled, kept, shift)  45.4 us
    pallas_call x1, Pallas kernels, on_device(): pl.pallas_call(correlate, grid=(planes,), out_shape=(shape((snaps - 1, pl...  7.05 us

profile of v1, /device:TPU:0, one launch (start us, length us, event | category | flops | bytes accessed | tf_op | source)
XLA Modules:
  0.0 53.1 jit_solution(17030732649853979425)
XLA Ops:
  0.6 45.4 %shard_map.50 = (f32[24,2,24,8,128]{4,3,2,1,0:T(8,128)}, f32[24,128]{1,0:T(8,128)}, f32[64,128]{1,0:T(8,128)}) custom-call(f32[8,4,16,8,256]{4,3,2,1,0:T(8,128)} %bitcast.4, s32[6]{0:T(128)} %kept.3, s32[7]{0:T(128)} %shift.3), custom_call_target="tpu_custom_call" | custom-call | tf_op jit(solution)/shard_map/pallas_call | solution.py:416
  46.0 7.1 %shard_map.51 = (f32[7,4,128,256]{3,2,1,0:T(8,128)}, f32[4,7]{1,0:T(4,128)}) custom-call(s32[6]{0:T(128)} %kept.3, s32[7]{0:T(128)} %shift.3, f32[6,4,2,192,128]{4,3,2,1,0:T(8,128)} %bitcast.3, f32[24,128]{1,0:T(8,128)} %get-tuple-element.8.inv, f32[64,128]{1,0:T(8,128)} %get-tuple-element.9.pair_sum), custom_call_target="tpu_custom_call" | custom-call | tf_op jit(solution)/shard_map/pallas_call | solution.py:420
